TPU v7x, 512 devices: a whole 4x4x16 slice. The times are simulated.
512 devices in a mesh: group: 8 (over x, core), dev: 64 (over z, y).
Axes of the slice: x: 4, y: 4, z: 16, core: 2. Of those that a mesh axis runs over, the one named last changes fastest.
Arguments:
- cam_jac: float32 [2, 9, 8, 262144], P(None, None, None, ('group', 'dev')), may hold values from -6 to 6
- lm_jac: float32 [2, 3, 8, 262144], P(None, None, None, ('group', 'dev')), may hold values from -6 to 6
- resid: float32 [2, 8, 262144], P(None, None, ('group', 'dev')), may hold values from -6 to 6
- cam_index: int32 [8, 262144], P(None, ('group', 'dev')), may hold values from 0 to 8191
Outputs:
- camera_step: float32 [9, 8192], P(None, 'dev')
- camera_residual: float32 [9, 8192], P(None, 'dev')
- landmark_step: float32 [3, 262144], P(None, ('group', 'dev'))
Inputs may be any that keep to these rules, and one draw needn't show every extreme that they name: `cam_index`: every observation names one of the 8192 cameras.
All inputs are finite; a program needn't handle non-finite values.
Results may differ from a plain program's by a relative error of at most 0.0003.
Values sent between devices are 32-bit elements; how exact they have to be, the bound alone decides.
A program may use at most 64 MiB of HBM per device.

v0:
```python
import jax
import jax.numpy as jnp
from jax import lax
from jax.sharding import PartitionSpec as P

CAM_DEV = 128
ITERS = 2
DAMPING = 1.0


def landmark_inverse(lm_jac):

    def entry(first, second):
        return jnp.sum(lm_jac[:, first] * lm_jac[:, second], axis=(0, 1))

    w_00 = entry(0, 0) + DAMPING
    w_11 = entry(1, 1) + DAMPING
    w_22 = entry(2, 2) + DAMPING
    w_01 = entry(0, 1)
    w_02 = entry(0, 2)
    w_12 = entry(1, 2)
    cof_00 = w_11 * w_22 - w_12 * w_12
    cof_01 = w_02 * w_12 - w_01 * w_22
    cof_02 = w_01 * w_12 - w_02 * w_11
    cof_11 = w_00 * w_22 - w_02 * w_02
    cof_12 = w_01 * w_02 - w_00 * w_12
    cof_22 = w_00 * w_11 - w_01 * w_01
    determinant = w_00 * cof_00 + w_01 * cof_01 + w_02 * cof_02
    rows = [
        jnp.stack([cof_00, cof_01, cof_02]),
        jnp.stack([cof_01, cof_11, cof_12]),
        jnp.stack([cof_02, cof_12, cof_22]),
    ]
    return jnp.stack(rows) / determinant[None, None]


def apply_inverse(inverse, vector):
    return jnp.sum(inverse * vector[None], axis=1)


def landmark_side(lm_jac, values):
    return jnp.sum(lm_jac * values[:, None], axis=(0, 2))


def back_project(lm_jac, landmark):
    return jnp.sum(lm_jac * landmark[None, :, None, :], axis=1)


def camera_apply(cam_jac, cam_values):
    return jnp.sum(cam_jac * cam_values[None], axis=1)


def camera_transpose(cam_jac, errors):
    return jnp.sum(cam_jac * errors[:, None], axis=0)


def to_cameras(values, cam_index, total_cams):
    flat_index = cam_index.reshape(-1)
    width = values.shape[0]

    def one_row(column):
        return jax.ops.segment_sum(column, flat_index, num_segments=total_cams)

    return jax.vmap(one_row)(values.reshape(width, -1))


def schur_obs(cam_jac, lm_jac, inverse, cam_values):
    applied = camera_apply(cam_jac, cam_values)
    landmark = apply_inverse(inverse, landmark_side(lm_jac, applied))
    return camera_transpose(cam_jac, applied - back_project(lm_jac, landmark))


def gather_cameras(tile):
    return lax.all_gather(tile, "dev", axis=1, tiled=True)


def reduce_cameras(terms):
    totals = lax.psum(terms, ("group", "dev"))
    width = terms.shape[1] // lax.axis_size("dev")
    return lax.dynamic_slice_in_dim(totals, lax.axis_index("dev") * width, width, 1)


def inner_product(left, right):
    return lax.psum(jnp.sum(left * right), "dev")


def body(cam_jac, lm_jac, resid, cam_index):
    total_cams = CAM_DEV * lax.axis_size("dev")
    inverse = landmark_inverse(lm_jac)
    land_rhs = apply_inverse(inverse, landmark_side(lm_jac, resid))
    errors = resid - back_project(lm_jac, land_rhs)
    stacked = jnp.concatenate(
        [camera_transpose(cam_jac, errors), jnp.sum(cam_jac * cam_jac, axis=0)], axis=0
    )
    summed = reduce_cameras(to_cameras(stacked, cam_index, total_cams))
    gradient = summed[:9]
    diagonal = summed[9:] + DAMPING
    residual = gradient
    precond = residual / diagonal
    direction = precond
    rz_now = inner_product(residual, precond)
    solution = jnp.zeros_like(gradient)
    for iteration in range(ITERS):
        whole = gather_cameras(direction)
        cam_values = jnp.take(whole, cam_index, axis=1)
        terms = to_cameras(schur_obs(cam_jac, lm_jac, inverse, cam_values), cam_index, total_cams)
        image = reduce_cameras(terms) + DAMPING * direction
        alpha = rz_now / inner_product(direction, image)
        solution = solution + alpha * direction
        residual = residual - alpha * image
        if iteration + 1 < ITERS:
            precond = residual / diagonal
            rz_next = inner_product(residual, precond)
            direction = precond + rz_next / rz_now * direction
            rz_now = rz_next
    whole_step = gather_cameras(solution)
    cam_obs = camera_apply(cam_jac, jnp.take(whole_step, cam_index, axis=1))
    landmark_step = land_rhs - apply_inverse(inverse, landmark_side(lm_jac, cam_obs))
    return (solution, residual, landmark_step)


def solution(mesh):
    in_specs = (
        P(None, None, None, ("group", "dev")),
        P(None, None, None, ("group", "dev")),
        P(None, None, ("group", "dev")),
        P(None, ("group", "dev")),
    )
    out_specs = (P(None, "dev"), P(None, "dev"), P(None, ("group", "dev")))
    return jax.shard_map(body, mesh=mesh, in_specs=in_specs, out_specs=out_specs, check_vma=False)
```

profile of v0, /device:TPU:8, one launch (start us, length us, event | category | flops | bytes accessed | tf_op | source)
XLA Modules:
  0.0 2390.0 jit_solution(14837299796872105308)
XLA Ops:
  11.5 1.0 multiply_reduce_fusion.6
  13.2 24.5 %scatter_custom_fusion = f32[18,8192]{0,1:T(8,128)} fusion(s32[4096]{0:T(1024)S(1)} %bitcast.43, f32[4096,18]{1,0:T(8,128)S(1)} %bitcast.38, f32[]{:T(128)} %constant.14.clone.1), kind=kCustom, calls=%fused_computation.13 | custom fusion | flops 73728 | bytes 589828 | tf_op jit(solution)/shard_map/vmap()/scatter-add | solution.py:62
  37.9 494.2 %all-reduce.5.cloned.1.call-done = f32[18,8192]{0,1:T(8,128)} async-done(((f32[18,8192]{0,1:T(8,128)}), f32[18,8192]{0,1:T(8,128)}) %all-reduce.5.cloned.1.call-update) | async-done | bytes 589840 | tf_op jit(solution)/shard_map/psum | solution.py:78
  533.1 111.9 %all_gather.9 = f32[9,8192]{0,1:T(8,128)} all-gather(f32[9,128]{0,1:T(8,128)S(1)} %fusion.7), channel_id=1, replica_groups=mesh['group'=8,'dev'=64] {'dev'}, dimensions={1}, use_global_device_ids=true | all-gather | bytes 299520 | tf_op jit(solution)/shard_map/all_gather | solution.py:74
  645.0 16.3 gather_fusion
  661.3 1.9 select_bitcast_fusion.2
  664.8 24.5 %scatter_custom_fusion.1 = f32[9,8192]{0,1:T(8,128)} fusion(s32[4096]{0:T(1024)S(1)} %bitcast.44, f32[4096,9]{1,0:T(8,128)S(1)} %bitcast.40, f32[]{:T(128)} %constant.14.clone.1), kind=kCustom, calls=%fused_computation.11 | custom fusion | flops 36864 | bytes 294916 | tf_op jit(solution)/shard_map/vmap()/scatter-add | solution.py:62
  689.4 488.0 %all-reduce.7.cloned.1.call-done = f32[9,8192]{0,1:T(8,128)} async-done(((f32[9,8192]{0,1:T(8,128)}), f32[9,8192]{0,1:T(8,128)}) %all-reduce.7.cloned.1.call-update) | async-done | bytes 294928 | tf_op jit(solution)/shard_map/psum | solution.py:78
  1177.4 1.6 multiply_reduce_fusion.16
  1179.0 139.5 %all-reduce = (f32[]{:T(128)}, f32[]{:T(128)}) all-reduce(f32[]{:T(128)} %get-tuple-element.22, f32[]{:T(128)} %get-tuple-element.21), channel_id=1, replica_groups=mesh['group'=8,'dev'=64] {'dev'}, use_global_device_ids=true, to_apply=%region_14.0 | all-reduce | flops 2 | bytes 16 | tf_op jit(solution)/shard_map/psum | solution.py:84
  1319.8 1.6 multiply_reduce_fusion.15
  1321.4 140.7 %psum.53 = f32[]{:T(128)} all-reduce(f32[]{:T(128)} %get-tuple-element.25), channel_id=1, replica_groups=mesh['group'=8,'dev'=64] {'dev'}, use_global_device_ids=true, to_apply=%region_25.27 | all-reduce | flops 1 | bytes 8 | tf_op jit(solution)/shard_map/psum | solution.py:84
  1463.5 1.0 multiply_add_fusion.1
  1464.5 110.5 %all_gather.10 = f32[9,8192]{0,1:T(8,128)} all-gather(f32[9,128]{0,1:T(8,128)S(1)} %multiply_add_fusion.1), channel_id=1, replica_groups=mesh['group'=8,'dev'=64] {'dev'}, dimensions={1}, use_global_device_ids=true | all-gather | bytes 299520 | tf_op jit(solution)/shard_map/all_gather | solution.py:74
  1575.0 16.3 gather_fusion.1
  1591.2 1.9 select_bitcast_fusion.1
  1594.6 24.5 %scatter_custom_fusion.2 = f32[9,8192]{0,1:T(8,128)} fusion(s32[4096]{0:T(1024)S(1)} %bitcast.45, f32[4096,9]{1,0:T(8,128)S(1)} %bitcast.39, f32[]{:T(128)} %constant.14.clone.1), kind=kCustom, calls=%fused_computation.9 | custom fusion | flops 36864 | bytes 294916 | tf_op jit(solution)/shard_map/vmap()/scatter-add | solution.py:62
  1619.2 488.2 %all-reduce.9.cloned.1.call-done = f32[9,8192]{0,1:T(8,128)} async-done(((f32[9,8192]{0,1:T(8,128)}), f32[9,8192]{0,1:T(8,128)}) %all-reduce.9.cloned.1.call-update) | async-done | bytes 294928 | tf_op jit(solution)/shard_map/psum | solution.py:78
  2107.4 1.5 multiply_reduce_fusion.14
  2108.9 139.4 %psum.55 = f32[]{:T(128)} all-reduce(f32[]{:T(128)} %multiply_reduce_fusion.14), channel_id=1, replica_groups=mesh['group'=8,'dev'=64] {'dev'}, use_global_device_ids=true, to_apply=%region_34.36 | all-reduce | flops 1 | bytes 8 | tf_op jit(solution)/shard_map/psum | solution.py:84
  2249.7 1.0 multiply_subtract_fusion
  2251.4 111.8 %all_gather.11 = f32[9,8192]{0,1:T(8,128)} all-gather(f32[9,128]{0,1:T(8,128)S(1)} %get-tuple-element.34), channel_id=1, replica_groups=mesh['group'=8,'dev'=64] {'dev'}, dimensions={1}, use_global_device_ids=true | all-gather | bytes 299520 | tf_op jit(solution)/shard_map/all_gather | solution.py:74
  2363.9 16.3 gather_fusion.2
  2380.2 1.9 select_bitcast_fusion
  (50 shorter events, 11.6 us)
Async XLA Ops:
  7.2 524.9 %all-reduce.5.cloned.1.call-start = ((), (), s32[]{:S(2)}) async-start(), calls=%async_computation | async-start | bytes 8388608 | tf_op jit(solution)/shard_map/psum | solution.py:78
  13.2 24.6 %copy-start.2 = (s32[8,512]{1,0:T(8,128)S(1)}, s32[8,512]{1,0:T(8,128)}, u32[]{:S(2)}) copy-start(s32[8,512]{1,0:T(8,128)} %param.9) | copy-start | bytes 49156
  37.8 1139.6 %all-reduce.7.cloned.1.call-start = ((), (), s32[]{:S(2)}) async-start(), calls=%async_computation.1 | async-start | bytes 8388608 | tf_op jit(solution)/shard_map/psum | solution.py:78
  645.0 18.9 copy-start
  645.0 19.0 copy-start.1
  689.3 1418.1 %all-reduce.9.cloned.1.call-start = ((), (), s32[]{:S(2)}) async-start(), calls=%async_computation.2 | async-start | bytes 8388608 | tf_op jit(solution)/shard_map/psum | solution.py:78
Sparse Core Ops, SparseCore 0:
  37.9 494.1 all-reduce.4
  689.4 487.8 all-reduce.6
  1619.3 488.0 all-reduce.8
where the time goes:
time: 2390 us
  waiting for transfers between devices  1470 us (62%)
  blocking collectives  754 us (32%)
  other arithmetic  92.8 us (4%)
  local copies, waits for them, and re-layouts  54.8 us (2%)
    psum x3, waiting for transfers between devices, reduce_cameras(): totals = lax.psum(terms, ('group', 'dev'))  1470 us
    psum x3, blocking collectives, inner_product(): return lax.psum(jnp.sum(left * right), 'dev')  420 us
    all_gather x3, blocking collectives, gather_cameras(): return lax.all_gather(tile, 'dev', axis=1, tiled=True)  334 us
    scatter-add x3, other arithmetic, one_row(): return jax.ops.segment_sum(column, flat_index, num_segments=total_cams)  73.6 us
  transfers between devices with their start and end apart: 3, of which 3 were waited for; matrix products, arithmetic and copies ran while one was open for 0% of the time, Pallas kernels for 0%

commit v1 on v0

--- a/solution.py
+++ b/solution.py
@@ -75,7 +75,7 @@
 
 
 def reduce_cameras(terms):
-    totals = lax.psum(terms, ("group", "dev"))
+    totals = lax.psum(lax.psum(terms, "group"), "dev")
     width = terms.shape[1] // lax.axis_size("dev")
     return lax.dynamic_slice_in_dim(totals, lax.axis_index("dev") * width, width, 1)
 

time: 2390 us -> 2060 us (0.86)
  the two profiles are of different devices: /device:TPU:8 before, /device:TPU:2 now
where the time goes in v1:
time: 2060 us
  waiting for transfers between devices  1140 us (55%)
  blocking collectives  754 us (37%)
  other arithmetic  92.7 us (4%)
  local copies, waits for them, and re-layouts  54.8 us (3%)
    psum x6, waiting for transfers between devices, reduce_cameras(): totals = lax.psum(lax.psum(terms, 'group'), 'dev')  1140 us
    psum x3, blocking collectives, inner_product(): return lax.psum(jnp.sum(left * right), 'dev')  421 us
    all_gather x3, blocking collectives, gather_cameras(): return lax.all_gather(tile, 'dev', axis=1, tiled=True)  334 us
    scatter-add x3, other arithmetic, one_row(): return jax.ops.segment_sum(column, flat_index, num_segments=total_cams)  73.6 us
  transfers between devices with their start and end apart: 6, of which 6 were waited for; matrix products, arithmetic and copies ran while one was open for 0% of the time, Pallas kernels for 0%

profile of v1, /device:TPU:2, one launch (start us, length us, event | category | flops | bytes accessed | tf_op | source)
XLA Modules:
  0.0 2061.2 jit_solution(17571016680688022028)
XLA Ops:
  13.2 24.5 %scatter_custom_fusion = f32[18,8192]{0,1:T(8,128)} fusion(s32[4096]{0:T(1024)S(1)} %bitcast.43, f32[4096,18]{1,0:T(8,128)S(1)} %bitcast.38, f32[]{:T(128)} %constant.14.clone.1), kind=kCustom, calls=%fused_computation.13 | custom fusion | flops 73728 | bytes 589828 | tf_op jit(solution)/shard_map/vmap()/scatter-add | solution.py:62
  37.8 90.0 %all-reduce.8.cloned.1.call-done = f32[18,8192]{0,1:T(8,128)} async-done(((f32[18,8192]{0,1:T(8,128)}), f32[18,8192]{0,1:T(8,128)}) %all-reduce.8.cloned.1.call-update) | async-done | bytes 589840 | tf_op jit(solution)/shard_map/psum | solution.py:78
  127.9 296.3 %all-reduce.10.cloned.1.call-done = f32[18,8192]{0,1:T(8,128)} async-done(((f32[18,8192]{0,1:T(8,128)}), f32[18,8192]{0,1:T(8,128)}) %all-reduce.10.cloned.1.call-update) | async-done | bytes 589840 | tf_op jit(solution)/shard_map/psum | solution.py:78
  425.1 111.5 %all_gather.9 = f32[9,8192]{0,1:T(8,128)} all-gather(f32[9,128]{0,1:T(8,128)S(1)} %fusion.7), channel_id=1, replica_groups=mesh['group'=8,'dev'=64] {'dev'}, dimensions={1}, use_global_device_ids=true | all-gather | bytes 299520 | tf_op jit(solution)/shard_map/all_gather | solution.py:74
  536.7 16.3 gather_fusion
  553.0 1.9 select_bitcast_fusion.2
  556.4 24.5 %scatter_custom_fusion.1 = f32[9,8192]{0,1:T(8,128)} fusion(s32[4096]{0:T(1024)S(1)} %bitcast.44, f32[4096,9]{1,0:T(8,128)S(1)} %bitcast.40, f32[]{:T(128)} %constant.14.clone.1), kind=kCustom, calls=%fused_computation.11 | custom fusion | flops 36864 | bytes 294916 | tf_op jit(solution)/shard_map/vmap()/scatter-add | solution.py:62
  581.0 80.9 %all-reduce.12.cloned.1.call-done = f32[9,8192]{0,1:T(8,128)} async-done(((f32[9,8192]{0,1:T(8,128)}), f32[9,8192]{0,1:T(8,128)}) %all-reduce.12.cloned.1.call-update) | async-done | bytes 294928 | tf_op jit(solution)/shard_map/psum | solution.py:78
  662.0 296.4 %all-reduce.14.cloned.1.call-done = f32[9,8192]{0,1:T(8,128)} async-done(((f32[9,8192]{0,1:T(8,128)}), f32[9,8192]{0,1:T(8,128)}) %all-reduce.14.cloned.1.call-update) | async-done | bytes 294928 | tf_op jit(solution)/shard_map/psum | solution.py:78
  958.4 1.6 multiply_reduce_fusion.16
  960.1 141.1 %all-reduce = (f32[]{:T(128)}, f32[]{:T(128)}) all-reduce(f32[]{:T(128)} %get-tuple-element.22, f32[]{:T(128)} %get-tuple-element.21), channel_id=1, replica_groups=mesh['group'=8,'dev'=64] {'dev'}, use_global_device_ids=true, to_apply=%region_15.0 | all-reduce | flops 2 | bytes 16 | tf_op jit(solution)/shard_map/psum | solution.py:84
  1102.5 1.6 multiply_reduce_fusion.15
  1104.1 138.8 %psum.76 = f32[]{:T(128)} all-reduce(f32[]{:T(128)} %get-tuple-element.25), channel_id=1, replica_groups=mesh['group'=8,'dev'=64] {'dev'}, use_global_device_ids=true, to_apply=%region_27.29 | all-reduce | flops 1 | bytes 8 | tf_op jit(solution)/shard_map/psum | solution.py:84
  1245.3 111.7 %all_gather.10 = f32[9,8192]{0,1:T(8,128)} all-gather(f32[9,128]{0,1:T(8,128)S(1)} %multiply_add_fusion.1), channel_id=1, replica_groups=mesh['group'=8,'dev'=64] {'dev'}, dimensions={1}, use_global_device_ids=true | all-gather | bytes 299520 | tf_op jit(solution)/shard_map/all_gather | solution.py:74
  1357.0 16.3 gather_fusion.1
  1373.3 1.9 select_bitcast_fusion.1
  1376.7 24.5 %scatter_custom_fusion.2 = f32[9,8192]{0,1:T(8,128)} fusion(s32[4096]{0:T(1024)S(1)} %bitcast.45, f32[4096,9]{1,0:T(8,128)S(1)} %bitcast.39, f32[]{:T(128)} %constant.14.clone.1), kind=kCustom, calls=%fused_computation.9 | custom fusion | flops 36864 | bytes 294916 | tf_op jit(solution)/shard_map/vmap()/scatter-add | solution.py:62
  1401.3 80.5 %all-reduce.16.cloned.1.call-done = f32[9,8192]{0,1:T(8,128)} async-done(((f32[9,8192]{0,1:T(8,128)}), f32[9,8192]{0,1:T(8,128)}) %all-reduce.16.cloned.1.call-update) | async-done | bytes 294928 | tf_op jit(solution)/shard_map/psum | solution.py:78
  1481.8 296.5 %all-reduce.18.cloned.1.call-done = f32[9,8192]{0,1:T(8,128)} async-done(((f32[9,8192]{0,1:T(8,128)}), f32[9,8192]{0,1:T(8,128)}) %all-reduce.18.cloned.1.call-update) | async-done | bytes 294928 | tf_op jit(solution)/shard_map/psum | solution.py:78
  1778.3 1.5 multiply_reduce_fusion.14
  1779.7 141.1 %psum.79 = f32[]{:T(128)} all-reduce(f32[]{:T(128)} %multiply_reduce_fusion.14), channel_id=1, replica_groups=mesh['group'=8,'dev'=64] {'dev'}, use_global_device_ids=true, to_apply=%region_37.39 | all-reduce | flops 1 | bytes 8 | tf_op jit(solution)/shard_map/psum | solution.py:84
  1923.9 110.3 %all_gather.11 = f32[9,8192]{0,1:T(8,128)} all-gather(f32[9,128]{0,1:T(8,128)S(1)} %get-tuple-element.34), channel_id=1, replica_groups=mesh['group'=8,'dev'=64] {'dev'}, dimensions={1}, use_global_device_ids=true | all-gather | bytes 299520 | tf_op jit(solution)/shard_map/all_gather | solution.py:74
  2034.8 16.3 gather_fusion.2
  2051.1 1.9 select_bitcast_fusion
  (59 shorter events, 14.9 us)
Async XLA Ops:
  7.2 120.6 %all-reduce.8.cloned.1.call-start = ((), (), s32[]{:S(2)}) async-start(), calls=%async_computation | async-start | bytes 8388608 | tf_op jit(solution)/shard_map/psum | solution.py:78
  37.7 90.1 %copy-start.2 = (s32[8,512]{1,0:T(8,128)S(1)}, s32[8,512]{1,0:T(8,128)}, u32[]{:S(2)}) copy-start(s32[8,512]{1,0:T(8,128)} %param.9) | copy-start | bytes 49156
  37.7 386.4 %all-reduce.10.cloned.1.call-start = ((), (), s32[]{:S(2)}) async-start(), calls=%async_computation.1 | async-start | bytes 8388608 | tf_op jit(solution)/shard_map/psum | solution.py:78
  127.7 534.2 %all-reduce.12.cloned.1.call-start = ((), (), s32[]{:S(2)}) async-start(), calls=%async_computation.2 | async-start | bytes 8388608 | tf_op jit(solution)/shard_map/psum | solution.py:78
  536.7 18.9 copy-start
  536.7 19.0 copy-start.1
  581.0 377.4 %all-reduce.14.cloned.1.call-start = ((), (), s32[]{:S(2)}) async-start(), calls=%async_computation.3 | async-start | bytes 8388608 | tf_op jit(solution)/shard_map/psum | solution.py:78
  661.9 819.8 %all-reduce.16.cloned.1.call-start = ((), (), s32[]{:S(2)}) async-start(), calls=%async_computation.4 | async-start | bytes 8388608 | tf_op jit(solution)/shard_map/psum | solution.py:78
  1401.3 377.0 %all-reduce.18.cloned.1.call-start = ((), (), s32[]{:S(2)}) async-start(), calls=%async_computation.5 | async-start | bytes 8388608 | tf_op jit(solution)/shard_map/psum | solution.py:78
Sparse Core Ops, SparseCore 0:
  37.8 89.8 all-reduce.7
  131.2 292.8 all-reduce.9
  581.1 80.7 all-reduce.11
  665.3 293.0 all-reduce.13
  1401.4 80.3 all-reduce.15
  1485.2 293.0 all-reduce.17
